TPU v7x, 32 devices: a whole 2x2x4 slice. The times are simulated.
32 devices in a mesh: grp: 2 (over y), gx: 4 (over z), gy: 2 (over x), gz: 2 (over core).
Axes of the slice: x: 2, y: 2, z: 4, core: 2. Of those that a mesh axis runs over, the one named last changes fastest.
Arguments:
- parcel_values: bfloat16 [6, 131072], P(None, ('grp', 'gx', 'gy', 'gz')), parts along dimension 1, may hold values from -2304 to 2304
- parcel_owner: int32 [131072, 1], P(('grp', 'gx', 'gy', 'gz')), parts along dimension 0, may hold values from 0 to 3; in each aligned block of 4096 rows (0 to 4095, 4096 to 8191, ...) at most 1536 rows name the same one
- parcel_cell: int32 [131072], P(('grp', 'gx', 'gy', 'gz')), parts along dimension 0, may hold values from 0 to 65535
- live_counts: int32 [32], P(('grp', 'gx', 'gy', 'gz')), parts along dimension 0, may hold values from 1 to 4096, 49152 in all
- fluid_state: bfloat16 [6, 256, 32, 256], P(None, ('grp', 'gx'), 'gy', 'gz'), parts along dimension 1, may hold values from -6 to 6
Outputs:
- coupled: bfloat16 [6, 256, 32, 256], P(None, ('grp', 'gx'), 'gy', 'gz'), parts along dimension 1
There are 2 independent parts, one for each index of `grp`. A program takes and returns all parts, laid end to end along the dimension named above; each array names one. Nothing has to cross between parts.
Inputs may be any that keep to these rules, and one draw needn't show every extreme that they name: `parcel_owner`: among the rows of one brick no streamwise index is named by more than 1536 rows; some brick names one exactly 1536 times. `parcel_cell`: cells are numbered (x * 16 + y) * 128 + z within the brick. `live_counts`: A brick's live parcels are its first rows; some brick has all rows live.
All inputs are finite; a program needn't handle non-finite values. No bound on the sum of `live_counts` on one device may be relied on, other than what follows from the above.
Results may differ from a plain program's by a relative error of at most 0.005.
Values may be sent and summed in bfloat16 or wider, within the bound.
A program may use at most 64 MiB of HBM per device.

v0:
```python
import jax
import jax.numpy as jnp
from jax import lax
from jax.sharding import PartitionSpec as P

REACH = 16
spread_cells = 12.0


def padded(shard, sides, width):
    for axis, dim in sides:
        size, length = (lax.axis_size(axis), shard.shape[dim])
        up = [(i, (i + 1) % size) for i in range(size)]
        down = [(j, i) for i, j in up]
        last = lax.slice_in_dim(shard, length - width, length, axis=dim)
        initial = lax.slice_in_dim(shard, 0, width, axis=dim)
        before = lax.ppermute(last, axis, up)
        after = lax.ppermute(initial, axis, down)
        shard = jnp.concatenate([before, shard, after], axis=dim)
    return shard


def tap_curve(offsets):
    tap_grid = jnp.arange(2 * REACH + 1).astype(jnp.float32)
    tap_sum = jnp.sum(
        jnp.exp(-(tap_grid - REACH) * (tap_grid - REACH) / (2.0 * spread_cells * spread_cells))
    )
    return (
        jnp.exp(-(offsets - REACH) * (offsets - REACH) / (2.0 * spread_cells * spread_cells))
        / tap_sum
    )


def banded(out_rows, in_rows, shift):
    row_ids = lax.broadcasted_iota(jnp.int32, (out_rows, in_rows), 0)
    col_ids = lax.broadcasted_iota(jnp.int32, (out_rows, in_rows), 1)
    offset_ids = col_ids - row_ids + shift
    inside = (offset_ids >= 0) & (offset_ids <= 2 * REACH)
    values = tap_curve(offset_ids.astype(jnp.float32)).astype(jnp.bfloat16)
    return jnp.where(inside, values, jnp.zeros_like(values))


def on_device(parcel_values, parcel_owner, parcel_cell, live_counts, fluid_state):
    channels, count_dev = parcel_values.shape
    width_x, width_y, width_z = (fluid_state.shape[1], fluid_state.shape[2], fluid_state.shape[3])
    owners = lax.axis_size("gx")
    capacity = 3 * count_dev // (2 * owners)
    owner_ids = parcel_owner[:, 0]
    local_rows = jnp.arange(count_dev, dtype=jnp.int32)
    is_live = local_rows < live_counts[0]
    owner_hits = (
        (owner_ids[:, None] == jnp.arange(owners, dtype=jnp.int32)[None, :]) & is_live[:, None]
    ).astype(jnp.int32)
    position = jnp.sum(jnp.cumsum(owner_hits, axis=0) * owner_hits, axis=1) - 1
    slot_index = jnp.where(is_live, owner_ids * capacity + position, owners * capacity)
    cell_xpart = (parcel_cell // (width_y * width_z)).astype(jnp.bfloat16)
    cell_ypart = (parcel_cell // width_z % width_y).astype(jnp.bfloat16)
    cell_low = (parcel_cell % width_z).astype(jnp.bfloat16)
    send_rows = jnp.concatenate(
        [parcel_values, cell_xpart[None, :], cell_ypart[None, :], cell_low[None, :]], axis=0
    )
    packed = (
        jnp.zeros((channels + 3, owners * capacity), jnp.bfloat16)
        .at[:, slot_index]
        .set(send_rows, mode="drop")
    )
    packed = packed.reshape(channels + 3, owners, capacity)
    arrived = lax.all_to_all(packed, "gx", split_axis=1, concat_axis=1, tiled=True).reshape(
        channels + 3, owners * capacity
    )
    slot_total = owners * capacity
    block_rows = min(1024, slot_total)
    plane_cells = width_x * width_y
    high_grid = jnp.arange(plane_cells, dtype=jnp.float32)
    low_grid = jnp.arange(width_z, dtype=jnp.float32)

    def deposit(step_index, summed):
        window = lax.dynamic_slice_in_dim(arrived, step_index * block_rows, block_rows, 1)
        high_ids = window[channels].astype(jnp.float32) * width_y + window[channels + 1].astype(
            jnp.float32
        )
        high_hot = (high_ids[:, None] == high_grid[None, :]).astype(jnp.bfloat16)
        low_hot = (window[channels + 2].astype(jnp.float32)[:, None] == low_grid[None, :]).astype(
            jnp.bfloat16
        )
        weighted = window[:channels][:, :, None] * low_hot[None, :, :]
        return summed + jnp.einsum(
            "sh,csz->chz", high_hot, weighted, preferred_element_type=jnp.float32
        )

    summed = lax.fori_loop(
        0,
        slot_total // block_rows,
        deposit,
        jnp.zeros((channels, plane_cells, width_z), jnp.float32),
    )
    source = summed.reshape(channels, width_x, width_y, width_z).astype(jnp.bfloat16)
    flat_source = source.reshape(channels, width_x, width_y * width_z)
    pencil = lax.all_to_all(flat_source, "gx", split_axis=2, concat_axis=1, tiled=True)
    full_x = pencil.shape[1]
    smoothed = jnp.einsum(
        "ij,cjk->cik", banded(full_x, full_x, REACH), pencil, preferred_element_type=jnp.float32
    ).astype(jnp.bfloat16)
    after_x = lax.all_to_all(smoothed, "gx", split_axis=1, concat_axis=2, tiled=True)
    after_x = after_x.reshape(channels, width_x, width_y, width_z)
    extended_y = padded(after_x, (("gy", 2),), REACH)
    after_y = jnp.einsum(
        "ij,cxjz->cxiz",
        banded(width_y, width_y + 2 * REACH, 0),
        extended_y,
        preferred_element_type=jnp.float32,
    ).astype(jnp.bfloat16)
    extended_z = padded(after_y, (("gz", 3),), REACH)
    smooth_z = jnp.einsum(
        "cxyj,ij->cxyi",
        extended_z,
        banded(width_z, width_z + 2 * REACH, 0),
        preferred_element_type=jnp.float32,
    )
    return (fluid_state.astype(jnp.float32) + smooth_z).astype(jnp.bfloat16)


def solution(mesh):
    in_specs = (
        P(None, ("grp", "gx", "gy", "gz")),
        P(("grp", "gx", "gy", "gz"), None),
        P(("grp", "gx", "gy", "gz")),
        P(("grp", "gx", "gy", "gz")),
        P(None, ("grp", "gx"), "gy", "gz"),
    )
    out_specs = P(None, ("grp", "gx"), "gy", "gz")
    return jax.shard_map(
        on_device, mesh=mesh, in_specs=in_specs, out_specs=out_specs, check_vma=False
    )
```

profile of v0, /device:TPU:0, one launch (start us, length us, event | category | flops | bytes accessed | tf_op | source)
XLA Modules:
  0.0 157.6 jit_solution(1705467644931148753)
XLA Ops:
  0.7 0.7 fusion.61
  1.4 1.2 reduce-window.6
  2.6 0.2 slice_reduce_fusion
  2.8 0.2 reduce-window.9
  3.0 0.1 add_bitcast_fusion
  3.1 0.8 fusion.53
  3.9 0.8 fusion.79
  4.8 0.9 maximum_bitcast_fusion
  5.7 0.5 copy.30
  6.3 11.4 %scatter_custom_fusion = bf16[9,6144]{0,1:T(8,128)(2,1)S(1)} fusion(s32[4096]{0:T(1024)S(1)} %bitcast.85, bf16[4096,9]{1,0:T(8,128)(2,1)S(1)} %copy.30, bf16[]{:T(256)} %constant.117.clone.1), kind=kCustom, calls=%fused_computation.36 | custom fusion | bytes 110594 | tf_op jit(solution)/shard_map/scatter | solution.py:65
  17.6 1.4 copy.31
  19.0 6.3 %all-to-all-start = ((bf16[9,4,1536]{2,0,1:T(8,128)(2,1)}), bf16[9,4,1536]{2,0,1:T(8,128)(2,1)S(1)}, u32[]{:S(2)}, u32[]{:S(2)}) async-start(bf16[9,4,1536]{2,0,1:T(8,128)(2,1)} %copy.31), calls=%async_computation | async-start | bytes 393216 | tf_op jit(solution)/shard_map/all_to_all | solution.py:68
  25.3 7.5 %all-to-all-done = bf16[9,4,1536]{2,0,1:T(8,128)(2,1)S(1)} async-done(((bf16[9,4,1536]{2,0,1:T(8,128)(2,1)}), bf16[9,4,1536]{2,0,1:T(8,128)(2,1)S(1)}, u32[]{:S(2)}, u32[]{:S(2)}) %all-to-all-start) | async-done | bytes 110624 | tf_op jit(solution)/shard_map/all_to_all | solution.py:68
  32.8 0.1 copy.32
  32.9 0.1 pad.10
  33.1 9.3 %while.14 = (s32[]{:T(128)}, f32[6,512,128]{1,2,0:T(8,128)S(1)}, bf16[9,6144]{1,0:T(8,128)(2,1)S(1)}, s32[]{:T(128)}, s32[]{:T(128)}, /*index=5*/s32[]{}, s32[]{:T(128)}, s32[]{:T(128)}, s32[]{}, s32[]{}) while((s32[]{:T(128)}, f32[6,512,128]{1,2,0:T(8,128)S(1)}, bf16[9,6144]{1,0:T(8,128)(2,1)S(1)}, s32[]{:T(128)}, s32[]{:T(128)}, ...), condition=%wide.region_5.6_spmd.clone, body=%wide.region_4.5_spmd.clone.sunk | while | flops 807670784 | bytes 3729625 | solution.py:91
  33.1 0.1 fusion.132
  33.2 0.1 fusion.131
  33.3 1.3 bitcast_add_fusion.2
  34.6 0.1 fusion.132
  34.7 0.1 fusion.131
  34.8 1.3 bitcast_add_fusion.2
  36.2 0.1 fusion.132
  36.3 0.1 fusion.131
  36.4 1.3 bitcast_add_fusion.2
  37.7 0.1 fusion.132
  37.8 0.1 fusion.131
  37.9 1.3 bitcast_add_fusion.2
  39.3 0.1 fusion.132
  39.4 0.1 fusion.131
  39.5 1.3 bitcast_add_fusion.2
  40.8 0.1 fusion.132
  40.9 0.1 fusion.131
  41.0 1.3 bitcast_add_fusion.2
  42.4 0.1 convert_element_type.119
  42.5 0.4 copy.33
  42.8 0.3 convert_element_type.120
  43.2 4.2 %copy.34 = bf16[6,32,2048]{1,0,2:T(8,128)(2,1)} copy(bf16[6,32,2048]{2,1,0:T(8,128)(2,1)S(1)} %convert_element_type.120) | data formatting | bytes 1572864 | tf_op jit(solution)/shard_map/convert_element_type | solution.py:97
  47.4 5.7 %reshape.138 = bf16[4,2,49152]{2,1,0:T(2,128)(2,1)} reshape(bf16[2048,6,32]{2,1,0:T(8,128)(2,1)} %bitcast.72) | data formatting | bytes 1572864
  53.1 3.5 %all-to-all-start.1 = ((bf16[4,2,49152]{2,1,0:T(2,128)(2,1)}), bf16[4,2,49152]{2,1,0:T(2,128)(2,1)S(1)}, u32[]{:S(2)}, u32[]{:S(2)}) async-start(bf16[4,2,49152]{2,1,0:T(2,128)(2,1)} %reshape.138), calls=%async_computation.1 | async-start | bytes 1572864 | tf_op jit(solution)/shard_map/all_to_all | solution.py:99
  56.6 0.6 fusion.104
  57.2 18.1 %all-to-all-done.1 = bf16[4,2,49152]{2,1,0:T(2,128)(2,1)S(1)} async-done(((bf16[4,2,49152]{2,1,0:T(2,128)(2,1)}), bf16[4,2,49152]{2,1,0:T(2,128)(2,1)S(1)}, u32[]{:S(2)}, u32[]{:S(2)}) %all-to-all-start.1) | async-done | bytes 786464 | tf_op jit(solution)/shard_map/all_to_all | solution.py:99
  75.3 4.2 %reshape.139 = bf16[2048,6,32]{2,1,0:T(8,128)(2,1)} reshape(bf16[4,2,49152]{2,1,0:T(2,128)(2,1)S(1)} %all-to-all-done.1) | data formatting | bytes 1572864
  79.5 4.5 %copy.48 = bf16[6,32,4,512]{3,2,1,0:T(4,128)(2,1)S(1)} copy(bf16[6,32,4,512]{1,0,3,2:T(8,128)(2,1)} %bitcast.73) | data formatting | bytes 1572864 | tf_op jit(solution)/shard_map/all_to_all | solution.py:99
  84.0 0.2 copy.36
  84.2 1.0 fusion.38
  85.2 0.9 copy.38
  86.1 27.7 %all_to_all.38 = bf16[6,128,512]{2,0,1:T(8,128)(2,1)S(1)} all-to-all(bf16[6,128,512]{2,0,1:T(8,128)(2,1)S(1)} %copy.38), channel_id=1, replica_groups=mesh['grp'=2,'gx'=4,'gy'=2,'gz'=2] {'gx'}, dimensions={1} | all-to-all | bytes 1572864 | tf_op jit(solution)/shard_map/all_to_all | solution.py:104
  113.8 0.6 copy.40
  114.4 0.3 reshape.120
  114.7 1.6 collective-permute-start
  116.2 0.5 collective-permute-start.1
  116.8 18.5 %collective-permute-done = bf16[6,32,16,128]{3,2,1,0:T(8,128)(2,1)S(1)} collective-permute-done((bf16[6,32,16,128]{3,2,1,0:T(8,128)(2,1)S(1)}, bf16[6,32,16,128]{3,2,1,0:T(8,128)(2,1)S(1)}, u32[]{:S(2)}, u32[]{:S(2)}) %collective-permute-start) | collective-permute-done | bytes 786464 | tf_op jit(solution)/shard_map/ppermute | solution.py:17
  135.2 14.4 %collective-permute-done.1 = bf16[6,32,16,128]{3,2,1,0:T(8,128)(2,1)S(1)} collective-permute-done((bf16[6,32,16,128]{3,2,1,0:T(8,128)(2,1)S(1)}, bf16[6,32,16,128]{3,2,1,0:T(8,128)(2,1)S(1)}, u32[]{:S(2)}, u32[]{:S(2)}) %collective-permute-start.1) | collective-permute-done | bytes 786464 | tf_op jit(solution)/shard_map/ppermute | solution.py:18
  149.7 1.1 fusion.35
  150.7 0.4 fusion.123
  151.1 0.6 copy.41
  151.8 0.6 copy.42
  152.5 0.5 collective-permute-start.3
  153.0 0.5 collective-permute-done.2
  153.5 0.6 copy.43
  154.2 0.2 collective-permute-done.3
  154.3 0.6 copy.44
  155.0 2.6 %add_convert_fusion = bf16[6,32,16,128]{3,2,1,0:T(8,128)(2,1)} fusion(bf16[6,32,16,128]{3,2,1,0:T(8,128)(2,1)S(1)} %copy-done.1, bf16[6,32,16,16]{3,2,1,0:T(8,128)(2,1)S(1)} %copy.44, bf16[6,32,16,128]{3,2,1,0:T(8,128)(2,1)S(1)} %fusion.35, bf16[6,32,16,16]{3,2,1,0:T(8,128)(2,1)S(1)} %copy.43, f32[]{:T(128)} %fusion.104), kind=kOutput, calls=%fused_computation.31 | convolution fusion | flops 130203648 | bytes 2555908 | tf_op jit(solution)/shard_map/cxyj,ij->cxyi/dot_general | solution.py:114
  (26 shorter events, 0.3 us)
Async XLA Ops:
  0.0 6.2 %copy-start = (s32[4096,1]{0,1:T(1,128)S(1)}, s32[4096,1]{0,1:T(1,128)}, u32[]{:S(2)}) copy-start(s32[4096,1]{0,1:T(1,128)} %param.8) | copy-start | bytes 49156
  19.0 13.8 %all-to-all-start = ((bf16[9,4,1536]{2,0,1:T(8,128)(2,1)}), bf16[9,4,1536]{2,0,1:T(8,128)(2,1)S(1)}, u32[]{:S(2)}, u32[]{:S(2)}) async-start(bf16[9,4,1536]{2,0,1:T(8,128)(2,1)} %copy.31), calls=%async_computation | async-start | bytes 393216 | tf_op jit(solution)/shard_map/all_to_all | solution.py:68
  53.1 22.2 %all-to-all-start.1 = ((bf16[4,2,49152]{2,1,0:T(2,128)(2,1)}), bf16[4,2,49152]{2,1,0:T(2,128)(2,1)S(1)}, u32[]{:S(2)}, u32[]{:S(2)}) async-start(bf16[4,2,49152]{2,1,0:T(2,128)(2,1)} %reshape.138), calls=%async_computation.1 | async-start | bytes 1572864 | tf_op jit(solution)/shard_map/all_to_all | solution.py:99
  114.7 20.5 %collective-permute-start = (bf16[6,32,16,128]{3,2,1,0:T(8,128)(2,1)S(1)}, bf16[6,32,16,128]{3,2,1,0:T(8,128)(2,1)S(1)}, u32[]{:S(2)}, u32[]{:S(2)}) collective-permute-start(bf16[6,32,16,128]{3,2,1,0:T(8,128)(2,1)S(1)} %reshape.120), channel_id=1, source_target_pairs={{0,2},{2,0},{1,3},{3,1},{4,6},{6,4},{5,7},{7,5},{8,10},{10,8},{9,1... | collective-permute-start | bytes 2359304 | tf_op jit(solution)/shard_map/ppermute | solution.py:17
  116.2 33.4 %collective-permute-start.1 = (bf16[6,32,16,128]{3,2,1,0:T(8,128)(2,1)S(1)}, bf16[6,32,16,128]{3,2,1,0:T(8,128)(2,1)S(1)}, u32[]{:S(2)}, u32[]{:S(2)}) collective-permute-start(bf16[6,32,16,128]{3,2,1,0:T(8,128)(2,1)S(1)} %reshape.120), channel_id=1, source_target_pairs={{2,0},{0,2},{3,1},{1,3},{6,4},{4,6},{7,5},{5,7},{10,8},{8,10},{11,... | collective-permute-start | bytes 2359304 | tf_op jit(solution)/shard_map/ppermute | solution.py:18
  151.7 1.8 %collective-permute-start.2 = (bf16[6,32,16,16]{1,3,2,0:T(8,128)(2,1)S(1)}, bf16[6,32,16,16]{1,3,2,0:T(8,128)(2,1)S(1)}, u32[]{:S(2)}, u32[]{:S(2)}) collective-permute-start(bf16[6,32,16,16]{1,3,2,0:T(8,128)(2,1)S(1)} %copy.41), channel_id=1, source_target_pairs={{0,1},{1,0},{2,3},{3,2},{4,5},{5,4},{6,7},{7,6},{8,9},{9,8},{10,11... | collective-permute-start | bytes 294920 | tf_op jit(solution)/shard_map/ppermute | solution.py:17
  151.8 3.2 %copy-start.1 = (bf16[6,32,16,128]{3,2,1,0:T(8,128)(2,1)S(1)}, bf16[6,32,16,128]{3,2,1,0:T(8,128)(2,1)}, u32[]{:S(2)}) copy-start(bf16[6,32,16,128]{3,2,1,0:T(8,128)(2,1)} %param.11) | copy-start | bytes 2359300
  152.5 1.9 %collective-permute-start.3 = (bf16[6,32,16,16]{1,3,2,0:T(8,128)(2,1)S(1)}, bf16[6,32,16,16]{1,3,2,0:T(8,128)(2,1)S(1)}, u32[]{:S(2)}, u32[]{:S(2)}) collective-permute-start(bf16[6,32,16,16]{1,3,2,0:T(8,128)(2,1)S(1)} %copy.42), channel_id=1, source_target_pairs={{1,0},{0,1},{3,2},{2,3},{5,4},{4,5},{7,6},{6,7},{9,8},{8,9},{11,10... | collective-permute-start | bytes 294920 | tf_op jit(solution)/shard_map/ppermute | solution.py:18
where the time goes:
time: 158 us
  waiting for transfers between devices  59.2 us (37%)
  local copies, waits for them, and re-layouts  37.9 us (24%)
  blocking collectives  27.7 us (18%)
  matrix products  12.6 us (8%)
  starting transfers between devices  12.5 us (8%)
  other arithmetic  6.49 us (4%)
    all_to_all x1, blocking collectives, on_device(): lax.all_to_all(smoothed, 'gx', split_axis=1, concat_axis=2, tiled=True)  27.7 us
    ppermute x2, waiting for transfers between devices, padded(): before = lax.ppermute(last, axis, up)  19 us
    all_to_all x1, waiting for transfers between devices, on_device(): lax.all_to_all(flat_source, 'gx', split_axis=2, concat_axis=1, tiled=True)  18.1 us
    ppermute x2, waiting for transfers between devices, padded(): after = lax.ppermute(initial, axis, down)  14.6 us
    scatter x1, local copies, waits for them, and re-layouts, on_device(): packed = jnp.zeros((channels + 3, owners * capacity), jnp.bfloat16).at[:,...  11.4 us
    unnamed x8, local copies, waits for them, and re-layouts  9.98 us
    dot_general x6, matrix products, deposit(): jnp.einsum('sh,csz->chz', high_hot, weighted, preferred_element_type=jnp....  7.91 us
    all_to_all x1, waiting for transfers between devices, on_device(): lax.all_to_all(packed, 'gx', split_axis=1, concat_axis=1, tiled=True)  7.51 us
  transfers between devices with their start and end apart: 6, of which 6 were waited for; matrix products, arithmetic and copies ran while one was open for 1% of the time, Pallas kernels for 0%

commit v1 on v0

--- a/solution.py
+++ b/solution.py
@@ -5,6 +5,30 @@
 
 REACH = 16
 spread_cells = 12.0
+
+
+def in_blocks(x, dim, count):
+    shape = x.shape
+    blocks = x.reshape(*shape[:dim], count, shape[dim] // count, *shape[dim + 1 :])
+    return jnp.moveaxis(blocks, dim, 0)
+
+
+def laid_out(pieces, dim):
+    pieces = jnp.moveaxis(pieces, 0, dim)
+    shape = pieces.shape
+    return pieces.reshape(*shape[:dim], shape[dim] * shape[dim + 1], *shape[dim + 2 :])
+
+
+def exchange_directly(shard, axis, split_dim, concat_dim):
+    size, index = (lax.axis_size(axis), lax.axis_index(axis))
+    pieces = in_blocks(shard, split_dim, size)
+    filled = pieces
+    for step in range(1, size):
+        target, source = ((index + step) % size, (index - step) % size)
+        sent = lax.dynamic_index_in_dim(pieces, target, 0)
+        partner_block = lax.ppermute(sent, axis, [(i, (i + step) % size) for i in range(size)])
+        filled = lax.dynamic_update_slice_in_dim(filled, partner_block, source, axis=0)
+    return laid_out(filled, concat_dim)
 
 
 def padded(shard, sides, width):
@@ -101,7 +125,7 @@
     smoothed = jnp.einsum(
         "ij,cjk->cik", banded(full_x, full_x, REACH), pencil, preferred_element_type=jnp.float32
     ).astype(jnp.bfloat16)
-    after_x = lax.all_to_all(smoothed, "gx", split_axis=1, concat_axis=2, tiled=True)
+    after_x = exchange_directly(smoothed, "gx", 1, 2)
     after_x = after_x.reshape(channels, width_x, width_y, width_z)
     extended_y = padded(after_x, (("gy", 2),), REACH)
     after_y = jnp.einsum(

time: 158 us -> 148 us (0.937); the launches traced: 158 us -> 145 us
  blocking collectives: 27.7 us -> 0 us
  waiting for transfers between devices: 59.2 us -> 71.1 us
  starting transfers between devices: 12.5 us -> 16.4 us
    all_to_all x1 -> x0, blocking collectives: 27.7 us -> none  [on_device(): lax.all_to_all(smoothed, 'gx', split_axis=1, concat_axis=2, tiled=True)]
    ppermute x0 -> x3, waiting for transfers between devices: none -> 12.4 us  [exchange_directly(): lax.ppermute(sent, axis, [(i, (i + step) % size) for i in range(size)])]
    ppermute x2, waiting for transfers between devices: 19 us -> 14.2 us  [padded(): before = lax.ppermute(last, axis, up)]
    ppermute x2, waiting for transfers between devices: 14.6 us -> 19 us  [padded(): after = lax.ppermute(initial, axis, down)]
    ppermute x0 -> x3, starting transfers between devices: none -> 3.87 us  [exchange_directly(): lax.ppermute(sent, axis, [(i, (i + step) % size) for i in range(size)])]
  transfers between devices with their start and end apart: 6 -> 9, of which waited for: 6 -> 8; matrix products, arithmetic and copies ran while one was open for 1% -> 1% of each run, Pallas kernels for 0% -> 0%
where the time goes in v1:
time: 148 us; the launch traced here: 145 us
  waiting for transfers between devices  71.1 us (48%)
  local copies, waits for them, and re-layouts  37.1 us (25%)
  starting transfers between devices  16.4 us (11%)
  matrix products  12.5 us (8%)
  other arithmetic  6.49 us (4%)
    ppermute x2, waiting for transfers between devices, padded(): after = lax.ppermute(initial, axis, down)  19 us
    all_to_all x1, waiting for transfers between devices, on_device(): lax.all_to_all(flat_source, 'gx', split_axis=2, concat_axis=1, tiled=True)  18 us
    ppermute x2, waiting for transfers between devices, padded(): before = lax.ppermute(last, axis, up)  14.2 us
    ppermute x3, waiting for transfers between devices, exchange_directly(): lax.ppermute(sent, axis, [(i, (i + step) % size) for i in range(size)])  12.4 us
    scatter x1, local copies, waits for them, and re-layouts, on_device(): packed = jnp.zeros((channels + 3, owners * capacity), jnp.bfloat16).at[:,...  11.4 us
    unnamed x8, local copies, waits for them, and re-layouts  9.97 us
    dot_general x6, matrix products, deposit(): jnp.einsum('sh,csz->chz', high_hot, weighted, preferred_element_type=jnp....  7.91 us
    all_to_all x1, waiting for transfers between devices, on_device(): lax.all_to_all(packed, 'gx', split_axis=1, concat_axis=1, tiled=True)  7.51 us
  transfers between devices with their start and end apart: 9, of which 8 were waited for; matrix products, arithmetic and copies ran while one was open for 1% of the time, Pallas kernels for 0%

profile of v1, /device:TPU:0, one launch (start us, length us, event | category | flops | bytes accessed | tf_op | source)
XLA Modules:
  0.0 144.9 jit_solution(562370054770898233)
XLA Ops:
  0.7 0.7 fusion.60
  1.4 1.2 reduce-window.6
  2.6 0.2 slice_reduce_fusion
  2.8 0.2 reduce-window.9
  3.0 0.1 add_bitcast_fusion
  3.1 0.8 fusion.52
  3.9 0.8 fusion.78
  4.8 0.9 maximum_bitcast_fusion
  5.7 0.5 copy.25
  6.3 11.4 %scatter_custom_fusion = bf16[9,6144]{0,1:T(8,128)(2,1)S(1)} fusion(s32[4096]{0:T(1024)S(1)} %bitcast.94, bf16[4096,9]{1,0:T(8,128)(2,1)S(1)} %copy.25, bf16[]{:T(256)} %constant.164.clone.1), kind=kCustom, calls=%fused_computation.35 | custom fusion | bytes 110594 | tf_op jit(solution)/shard_map/scatter | solution.py:89
  17.6 1.4 copy.26
  19.0 6.3 %all-to-all-start = ((bf16[9,4,1536]{2,0,1:T(8,128)(2,1)}), bf16[9,4,1536]{2,0,1:T(8,128)(2,1)S(1)}, u32[]{:S(2)}, u32[]{:S(2)}) async-start(bf16[9,4,1536]{2,0,1:T(8,128)(2,1)} %copy.26), calls=%async_computation | async-start | bytes 393216 | tf_op jit(solution)/shard_map/all_to_all | solution.py:92
  25.3 7.5 %all-to-all-done = bf16[9,4,1536]{2,0,1:T(8,128)(2,1)S(1)} async-done(((bf16[9,4,1536]{2,0,1:T(8,128)(2,1)}), bf16[9,4,1536]{2,0,1:T(8,128)(2,1)S(1)}, u32[]{:S(2)}, u32[]{:S(2)}) %all-to-all-start) | async-done | bytes 110624 | tf_op jit(solution)/shard_map/all_to_all | solution.py:92
  32.8 0.1 copy.27
  33.1 9.3 %while.14 = (s32[]{:T(128)}, f32[6,512,128]{1,2,0:T(8,128)S(1)}, bf16[9,6144]{1,0:T(8,128)(2,1)S(1)}, s32[]{:T(128)}, s32[]{:T(128)}, /*index=5*/s32[]{}, s32[]{:T(128)}, s32[]{:T(128)}, s32[]{}, s32[]{}) while((s32[]{:T(128)}, f32[6,512,128]{1,2,0:T(8,128)S(1)}, bf16[9,6144]{1,0:T(8,128)(2,1)S(1)}, s32[]{:T(128)}, s32[]{:T(128)}, ...), condition=%wide.region_5.6_spmd.clone, body=%wide.region_4.5_spmd.clone.sunk | while | flops 807670784 | bytes 3729633 | solution.py:115
  33.1 0.1 fusion.130
  33.2 0.1 fusion.131
  33.3 1.3 bitcast_add_fusion.2
  34.6 0.1 fusion.130
  34.7 0.1 fusion.131
  34.8 1.3 bitcast_add_fusion.2
  36.2 0.1 fusion.130
  36.3 0.1 fusion.131
  36.4 1.3 bitcast_add_fusion.2
  37.7 0.1 fusion.130
  37.8 0.1 fusion.131
  37.9 1.3 bitcast_add_fusion.2
  39.3 0.1 fusion.130
  39.4 0.1 fusion.131
  39.5 1.3 bitcast_add_fusion.2
  40.8 0.1 fusion.130
  41.0 1.3 bitcast_add_fusion.2
  42.4 0.1 convert_element_type.119
  42.5 0.4 copy.28
  42.8 0.3 convert_element_type.120
  43.2 4.2 %copy.29 = bf16[6,32,2048]{1,0,2:T(8,128)(2,1)} copy(bf16[6,32,2048]{2,1,0:T(8,128)(2,1)S(1)} %convert_element_type.120) | data formatting | bytes 1572864 | tf_op jit(solution)/shard_map/convert_element_type | solution.py:121
  47.4 5.7 %reshape.140 = bf16[4,2,49152]{2,1,0:T(2,128)(2,1)} reshape(bf16[2048,6,32]{2,1,0:T(8,128)(2,1)} %bitcast.79) | data formatting | bytes 1572864
  53.1 3.5 %all-to-all-start.1 = ((bf16[4,2,49152]{2,1,0:T(2,128)(2,1)}), bf16[4,2,49152]{2,1,0:T(2,128)(2,1)S(1)}, u32[]{:S(2)}, u32[]{:S(2)}) async-start(bf16[4,2,49152]{2,1,0:T(2,128)(2,1)} %reshape.140), calls=%async_computation.1 | async-start | bytes 1572864 | tf_op jit(solution)/shard_map/all_to_all | solution.py:123
  56.7 0.6 fusion.106
  57.3 18.0 %all-to-all-done.1 = bf16[4,2,49152]{2,1,0:T(2,128)(2,1)S(1)} async-done(((bf16[4,2,49152]{2,1,0:T(2,128)(2,1)}), bf16[4,2,49152]{2,1,0:T(2,128)(2,1)S(1)}, u32[]{:S(2)}, u32[]{:S(2)}) %all-to-all-start.1) | async-done | bytes 786464 | tf_op jit(solution)/shard_map/all_to_all | solution.py:123
  75.3 4.2 %reshape.141 = bf16[2048,6,32]{2,1,0:T(8,128)(2,1)} reshape(bf16[4,2,49152]{2,1,0:T(2,128)(2,1)S(1)} %all-to-all-done.1) | data formatting | bytes 1572864
  79.5 4.5 %copy.39 = bf16[6,32,4,512]{3,2,1,0:T(4,128)(2,1)S(1)} copy(bf16[6,32,4,512]{1,0,3,2:T(8,128)(2,1)} %bitcast.80) | data formatting | bytes 1572864 | tf_op jit(solution)/shard_map/all_to_all | solution.py:123
  84.0 0.2 copy.31
  84.2 1.0 convolution_convert_fusion
  85.3 2.0 %collective-permute-start.1 = (bf16[1,6,32,512]{3,2,0,1:T(8,128)(2,1)S(1)}, bf16[1,6,32,512]{3,2,0,1:T(8,128)(2,1)S(1)}, u32[]{:S(2)}, u32[]{:S(2)}) collective-permute-start(bf16[1,6,32,512]{3,2,0,1:T(8,128)(2,1)S(1)} %get-tuple-element.125), channel_id=1, source_target_pairs={{0,8},{4,12},{8,0},{12,4},{1,9},{5,13},{9,1},{13,5},{2,10},{6,14},... | collective-permute-start | bytes 589832 | tf_op jit(solution)/shard_map/ppermute | solution.py:29
  87.3 1.8 %collective-permute-start.2 = (bf16[1,6,32,512]{3,2,0,1:T(8,128)(2,1)S(1)}, bf16[1,6,32,512]{3,2,0,1:T(8,128)(2,1)S(1)}, u32[]{:S(2)}, u32[]{:S(2)}) collective-permute-start(bf16[1,6,32,512]{3,2,0,1:T(8,128)(2,1)S(1)} %get-tuple-element.124), channel_id=1, source_target_pairs={{0,12},{4,0},{8,4},{12,8},{1,13},{5,1},{9,5},{13,9},{2,14},{6,2},{... | collective-permute-start | bytes 589832 | tf_op jit(solution)/shard_map/ppermute | solution.py:29
  89.1 5.9 %collective-permute-done = bf16[1,6,32,512]{3,2,0,1:T(8,128)(2,1)S(1)} collective-permute-done((bf16[1,6,32,512]{3,2,0,1:T(8,128)(2,1)S(1)}, bf16[1,6,32,512]{3,2,0,1:T(8,128)(2,1)S(1)}, u32[]{:S(2)}, u32[]{:S(2)}) %collective-permute-start) | collective-permute-done | bytes 196640 | tf_op jit(solution)/shard_map/ppermute | solution.py:29
  95.0 6.5 %collective-permute-done.1 = bf16[1,6,32,512]{3,2,0,1:T(8,128)(2,1)S(1)} collective-permute-done((bf16[1,6,32,512]{3,2,0,1:T(8,128)(2,1)S(1)}, bf16[1,6,32,512]{3,2,0,1:T(8,128)(2,1)S(1)}, u32[]{:S(2)}, u32[]{:S(2)}) %collective-permute-start.1) | collective-permute-done | bytes 196640 | tf_op jit(solution)/shard_map/ppermute | solution.py:29
  101.6 0.6 copy.32
  102.2 0.3 reshape_reshape.3
  102.5 1.6 %collective-permute-start.4 = (bf16[6,32,16,128]{3,2,1,0:T(8,128)(2,1)S(1)}, bf16[6,32,16,128]{3,2,1,0:T(8,128)(2,1)S(1)}, u32[]{:S(2)}, u32[]{:S(2)}) collective-permute-start(bf16[6,32,16,128]{3,2,1,0:T(8,128)(2,1)S(1)} %reshape_reshape.3), channel_id=1, source_target_pairs={{2,0},{0,2},{3,1},{1,3},{6,4},{4,6},{7,5},{5,7},{10,8},{8,10},{11,... | collective-permute-start | bytes 2359304 | tf_op jit(solution)/shard_map/ppermute | solution.py:42
  104.1 0.5 collective-permute-start.3
  104.6 18.5 %collective-permute-done.4 = bf16[6,32,16,128]{3,2,1,0:T(8,128)(2,1)S(1)} collective-permute-done((bf16[6,32,16,128]{3,2,1,0:T(8,128)(2,1)S(1)}, bf16[6,32,16,128]{3,2,1,0:T(8,128)(2,1)S(1)}, u32[]{:S(2)}, u32[]{:S(2)}) %collective-permute-start.4) | collective-permute-done | bytes 786464 | tf_op jit(solution)/shard_map/ppermute | solution.py:42
  123.1 14.0 %collective-permute-done.3 = bf16[6,32,16,128]{3,2,1,0:T(8,128)(2,1)S(1)} collective-permute-done((bf16[6,32,16,128]{3,2,1,0:T(8,128)(2,1)S(1)}, bf16[6,32,16,128]{3,2,1,0:T(8,128)(2,1)S(1)}, u32[]{:S(2)}, u32[]{:S(2)}) %collective-permute-start.3) | collective-permute-done | bytes 786464 | tf_op jit(solution)/shard_map/ppermute | solution.py:41
  137.0 1.1 fusion.35
  138.1 0.4 fusion.122
  138.5 0.6 copy.34
  139.2 0.6 copy.33
  139.8 0.5 collective-permute-start.5
  140.3 0.5 collective-permute-done.6
  140.9 0.6 copy.36
  141.5 0.2 collective-permute-done.5
  141.7 0.6 copy.35
  142.3 2.6 %add_convert_fusion = bf16[6,32,16,128]{3,2,1,0:T(8,128)(2,1)} fusion(bf16[6,32,16,128]{3,2,1,0:T(8,128)(2,1)S(1)} %copy-done.1, bf16[6,32,16,16]{3,2,1,0:T(8,128)(2,1)S(1)} %copy.36, bf16[6,32,16,128]{3,2,1,0:T(8,128)(2,1)S(1)} %fusion.35, bf16[6,32,16,16]{3,2,1,0:T(8,128)(2,1)S(1)} %copy.35, f32[]{:T(128)} %fusion.106), kind=kOutput, calls=%fused_computation.31 | convolution fusion | flops 130203648 | bytes 2555908 | tf_op jit(solution)/shard_map/cxyj,ij->cxyi/dot_general | solution.py:138
  (34 shorter events, 0.6 us)
Async XLA Ops:
  0.0 6.2 %copy-start = (s32[4096,1]{0,1:T(1,128)S(1)}, s32[4096,1]{0,1:T(1,128)}, u32[]{:S(2)}) copy-start(s32[4096,1]{0,1:T(1,128)} %param.8) | copy-start | bytes 49156
  19.0 13.8 %all-to-all-start = ((bf16[9,4,1536]{2,0,1:T(8,128)(2,1)}), bf16[9,4,1536]{2,0,1:T(8,128)(2,1)S(1)}, u32[]{:S(2)}, u32[]{:S(2)}) async-start(bf16[9,4,1536]{2,0,1:T(8,128)(2,1)} %copy.26), calls=%async_computation | async-start | bytes 393216 | tf_op jit(solution)/shard_map/all_to_all | solution.py:92
  53.1 22.2 %all-to-all-start.1 = ((bf16[4,2,49152]{2,1,0:T(2,128)(2,1)}), bf16[4,2,49152]{2,1,0:T(2,128)(2,1)S(1)}, u32[]{:S(2)}, u32[]{:S(2)}) async-start(bf16[4,2,49152]{2,1,0:T(2,128)(2,1)} %reshape.140), calls=%async_computation.1 | async-start | bytes 1572864 | tf_op jit(solution)/shard_map/all_to_all | solution.py:123
  85.2 9.8 %collective-permute-start = (bf16[1,6,32,512]{3,2,0,1:T(8,128)(2,1)S(1)}, bf16[1,6,32,512]{3,2,0,1:T(8,128)(2,1)S(1)}, u32[]{:S(2)}, u32[]{:S(2)}) collective-permute-start(bf16[1,6,32,512]{3,2,0,1:T(8,128)(2,1)S(1)} %get-tuple-element.126), channel_id=1, source_target_pairs={{0,4},{4,8},{8,12},{12,0},{1,5},{5,9},{9,13},{13,1},{2,6},{6,10},{... | collective-permute-start | bytes 589832 | tf_op jit(solution)/shard_map/ppermute | solution.py:29
  85.3 16.3 %collective-permute-start.1 = (bf16[1,6,32,512]{3,2,0,1:T(8,128)(2,1)S(1)}, bf16[1,6,32,512]{3,2,0,1:T(8,128)(2,1)S(1)}, u32[]{:S(2)}, u32[]{:S(2)}) collective-permute-start(bf16[1,6,32,512]{3,2,0,1:T(8,128)(2,1)S(1)} %get-tuple-element.125), channel_id=1, source_target_pairs={{0,8},{4,12},{8,0},{12,4},{1,9},{5,13},{9,1},{13,5},{2,10},{6,14},... | collective-permute-start | bytes 589832 | tf_op jit(solution)/shard_map/ppermute | solution.py:29
  87.3 14.3 %collective-permute-start.2 = (bf16[1,6,32,512]{3,2,0,1:T(8,128)(2,1)S(1)}, bf16[1,6,32,512]{3,2,0,1:T(8,128)(2,1)S(1)}, u32[]{:S(2)}, u32[]{:S(2)}) collective-permute-start(bf16[1,6,32,512]{3,2,0,1:T(8,128)(2,1)S(1)} %get-tuple-element.124), channel_id=1, source_target_pairs={{0,12},{4,0},{8,4},{12,8},{1,13},{5,1},{9,5},{13,9},{2,14},{6,2},{... | collective-permute-start | bytes 589832 | tf_op jit(solution)/shard_map/ppermute | solution.py:29
  102.5 20.5 %collective-permute-start.4 = (bf16[6,32,16,128]{3,2,1,0:T(8,128)(2,1)S(1)}, bf16[6,32,16,128]{3,2,1,0:T(8,128)(2,1)S(1)}, u32[]{:S(2)}, u32[]{:S(2)}) collective-permute-start(bf16[6,32,16,128]{3,2,1,0:T(8,128)(2,1)S(1)} %reshape_reshape.3), channel_id=1, source_target_pairs={{2,0},{0,2},{3,1},{1,3},{6,4},{4,6},{7,5},{5,7},{10,8},{8,10},{11,... | collective-permute-start | bytes 2359304 | tf_op jit(solution)/shard_map/ppermute | solution.py:42
  104.1 33.0 %collective-permute-start.3 = (bf16[6,32,16,128]{3,2,1,0:T(8,128)(2,1)S(1)}, bf16[6,32,16,128]{3,2,1,0:T(8,128)(2,1)S(1)}, u32[]{:S(2)}, u32[]{:S(2)}) collective-permute-start(bf16[6,32,16,128]{3,2,1,0:T(8,128)(2,1)S(1)} %reshape_reshape.3), channel_id=1, source_target_pairs={{0,2},{2,0},{1,3},{3,1},{4,6},{6,4},{5,7},{7,5},{8,10},{10,8},{9,1... | collective-permute-start | bytes 2359304 | tf_op jit(solution)/shard_map/ppermute | solution.py:41
  139.1 1.8 %collective-permute-start.6 = (bf16[6,32,16,16]{1,3,2,0:T(8,128)(2,1)S(1)}, bf16[6,32,16,16]{1,3,2,0:T(8,128)(2,1)S(1)}, u32[]{:S(2)}, u32[]{:S(2)}) collective-permute-start(bf16[6,32,16,16]{1,3,2,0:T(8,128)(2,1)S(1)} %copy.34), channel_id=1, source_target_pairs={{1,0},{0,1},{3,2},{2,3},{5,4},{4,5},{7,6},{6,7},{9,8},{8,9},{11,10... | collective-permute-start | bytes 294920 | tf_op jit(solution)/shard_map/ppermute | solution.py:42
  139.2 3.2 %copy-start.1 = (bf16[6,32,16,128]{3,2,1,0:T(8,128)(2,1)S(1)}, bf16[6,32,16,128]{3,2,1,0:T(8,128)(2,1)}, u32[]{:S(2)}) copy-start(bf16[6,32,16,128]{3,2,1,0:T(8,128)(2,1)} %param.11) | copy-start | bytes 2359300
  139.8 1.9 %collective-permute-start.5 = (bf16[6,32,16,16]{1,3,2,0:T(8,128)(2,1)S(1)}, bf16[6,32,16,16]{1,3,2,0:T(8,128)(2,1)S(1)}, u32[]{:S(2)}, u32[]{:S(2)}) collective-permute-start(bf16[6,32,16,16]{1,3,2,0:T(8,128)(2,1)S(1)} %copy.33), channel_id=1, source_target_pairs={{0,1},{1,0},{2,3},{3,2},{4,5},{5,4},{6,7},{7,6},{8,9},{9,8},{10,11... | collective-permute-start | bytes 294920 | tf_op jit(solution)/shard_map/ppermute | solution.py:41
